TPU v7x, 32 devices: a whole 2x2x4 slice. The times are simulated.
32 devices in a mesh: rep: 16 (over z, y, x), shard: 2 (over core).
Axes of the slice: x: 2, y: 2, z: 4, core: 2. Of those that a mesh axis runs over, the one named last changes fastest.
Arguments:
- tokens: bfloat16 [32, 1024, 640], P(('rep', 'shard')), may hold values from -6 to 6
- segments: int32 [32, 1024], P(('rep', 'shard')), may hold values from 0 to 3, never falling along the last dimension, each value on 1 to 512 neighbouring positions
- w_query: bfloat16 [640, 1024], P('shard'), may hold values from -0.25 to 0.25
- w_key: bfloat16 [640, 256], P('shard'), may hold values from -0.25 to 0.25
- w_value: bfloat16 [640, 256], P('shard'), may hold values from -0.25 to 0.25
- w_output: bfloat16 [1024, 640], P('shard'), may hold values from -0.375 to 0.375
- w_gate: bfloat16 [640, 2048], P('shard'), may hold values from -0.25 to 0.25
- w_up: bfloat16 [640, 2048], P('shard'), may hold values from -0.25 to 0.25
- w_down: bfloat16 [2048, 640], P('shard'), may hold values from -0.125 to 0.125
- gain_input: bfloat16 [640], P('shard'), may hold values from 0.099609375 to 1.8984375
- gain_query: bfloat16 [256], P('shard'), may hold values from 0.099609375 to 1.8984375
- gain_key: bfloat16 [256], P('shard'), may hold values from 0.099609375 to 1.8984375
- gain_attend: bfloat16 [640], P('shard'), may hold values from 0.099609375 to 1.8984375
- gain_ffn: bfloat16 [640], P('shard'), may hold values from 0.099609375 to 1.8984375
- gain_post: bfloat16 [640], P('shard'), may hold values from 0.099609375 to 1.8984375
- cotangent: bfloat16 [32, 1024, 640], P(('rep', 'shard')), may hold values from -6 to 6
Outputs:
- outputs: bfloat16 [32, 1024, 640], P(('rep', 'shard'))
- grad_tokens: bfloat16 [32, 1024, 640], P(('rep', 'shard'))
- grad_query: float32 [640, 1024], P('shard')
- grad_key: float32 [640, 256], P('shard')
- grad_value: float32 [640, 256], P('shard')
- grad_output: float32 [1024, 640], P('shard')
- grad_gate: float32 [640, 2048], P('shard')
- grad_up: float32 [640, 2048], P('shard')
- grad_down: float32 [2048, 640], P('shard')
- grad_gain_input: float32 [640], P('shard')
- grad_gain_query: float32 [256], P('shard')
- grad_gain_key: float32 [256], P('shard')
- grad_gain_attend: float32 [640], P('shard')
- grad_gain_ffn: float32 [640], P('shard')
- grad_gain_post: float32 [640], P('shard')
Inputs may be any that keep to these rules, and one draw needn't show every extreme that they name: `segments`: within each sequence segment numbers never fall; each document has 1 to 512 tokens, and one has exactly 512.
All inputs are finite; a program needn't handle non-finite values.
Results may differ from a plain program's by a relative error of at most 0.025.
Values may be sent and summed in bfloat16 or wider, within the bound.
A program may use at most 192 MiB of HBM per device.

v0:
```python
import functools

import jax
import jax.numpy as jnp
from jax import lax
from jax.sharding import PartitionSpec as P

EPS = 1e-06
THETA = 1000000.0
BLOCK = 256
DOC_MOST = 512


def norm_rows(values, gain):
    return values * lax.rsqrt(jnp.mean(values * values, axis=-1, keepdims=True) + EPS) * gain


def rotary(values, cosine, sine_part):
    halfway = values.shape[-1] // 2
    front = values[..., :halfway]
    behind = values[..., halfway:]
    return jnp.concatenate(
        [front * cosine - behind * sine_part, behind * cosine + front * sine_part], axis=-1
    )


def rotary_tables(segment, width):
    length = segment.shape[0]
    indices = jnp.arange(length, dtype=jnp.int32)
    change = jnp.concatenate([jnp.ones((1,), dtype=bool), segment[1:] != segment[:-1]])
    starts = lax.cummax(jnp.where(change, indices, 0), axis=0)
    position = (indices - starts).astype(jnp.float32)
    halfway = width // 2
    frequency = THETA ** (-(2.0 * jnp.arange(halfway, dtype=jnp.float32)) / (2.0 * halfway))
    turned = position[:, None] * frequency[None, :]
    return (jnp.cos(turned), jnp.sin(turned))


def glu_part(gate_out, upward):
    return jax.nn.gelu(gate_out, approximate=True) * upward


def block_mask(segment, start, low, high):
    rows_idx = jnp.arange(start, high, dtype=jnp.int32)
    cols_idx = jnp.arange(low, high, dtype=jnp.int32)
    same_doc = segment[start:high][:, None] == segment[low:high][None, :]
    return same_doc & (rows_idx[:, None] >= cols_idx[None, :])


def forward(inputs, segment, mats):
    (
        w_query,
        w_key,
        w_value,
        w_output,
        w_gate,
        w_up,
        w_down,
        gain_input,
        gain_query,
        gain_key,
        gain_attend,
        gain_ffn,
        gain_post,
    ) = mats
    length = inputs.shape[0]
    width = w_key.shape[1]
    heads = w_query.shape[1] // width
    block = min(BLOCK, length)
    cosine, sine_part = rotary_tables(segment, width)
    normed = norm_rows(inputs, gain_input.astype(jnp.float32)).astype(jnp.bfloat16)
    query_raw = jnp.dot(normed, w_query, preferred_element_type=jnp.float32).reshape(
        length, heads, width
    )
    key_raw = jnp.dot(normed, w_key, preferred_element_type=jnp.float32)
    values = jnp.dot(normed, w_value, preferred_element_type=jnp.float32).astype(jnp.bfloat16)
    queries = (
        rotary(
            norm_rows(query_raw, gain_query.astype(jnp.float32)),
            cosine[:, None, :],
            sine_part[:, None, :],
        )
        * width ** (-0.5)
    ).astype(jnp.bfloat16)
    keys_rot = rotary(norm_rows(key_raw, gain_key.astype(jnp.float32)), cosine, sine_part).astype(
        jnp.bfloat16
    )
    pieces = []
    kept_probs = []
    for start in range(0, length, block):
        low = max(0, start - DOC_MOST)
        high = start + block
        scores = jnp.einsum(
            "lhd,md->hlm",
            queries[start:high],
            keys_rot[low:high],
            preferred_element_type=jnp.float32,
        )
        allowed = block_mask(segment, start, low, high)
        scores = jnp.where(allowed[None], scores, -1e30)
        largest = jnp.max(scores, axis=-1, keepdims=True)
        expd = jnp.exp(scores - largest)
        totals = jnp.sum(expd, axis=-1, keepdims=True)
        probabilities = (expd / totals).astype(jnp.bfloat16)
        kept_probs.append(probabilities)
        pieces.append(
            jnp.einsum(
                "hlm,md->lhd", probabilities, values[low:high], preferred_element_type=jnp.float32
            )
        )
    attended = jnp.concatenate(pieces, axis=0).astype(jnp.bfloat16).reshape(length, heads * width)
    branch = jnp.dot(attended, w_output, preferred_element_type=jnp.float32)
    middle = inputs + norm_rows(branch, gain_attend.astype(jnp.float32))
    normed_two = norm_rows(middle, gain_ffn.astype(jnp.float32)).astype(jnp.bfloat16)
    gate_out = jnp.dot(normed_two, w_gate, preferred_element_type=jnp.float32)
    upward = jnp.dot(normed_two, w_up, preferred_element_type=jnp.float32)
    hidden = glu_part(gate_out, upward).astype(jnp.bfloat16)
    branch_two = jnp.dot(hidden, w_down, preferred_element_type=jnp.float32)
    result = middle + norm_rows(branch_two, gain_post.astype(jnp.float32))
    kept = (
        inputs,
        segment,
        cosine,
        sine_part,
        normed,
        query_raw,
        key_raw,
        values,
        queries,
        keys_rot,
        kept_probs,
        attended,
        branch,
        middle,
        normed_two,
        gate_out,
        upward,
        hidden,
        branch_two,
    )
    return (result, kept)


def backward_ffn(kept, incoming, mats):
    (
        w_query,
        w_key,
        w_value,
        w_output,
        w_gate,
        w_up,
        w_down,
        gain_input,
        gain_query,
        gain_key,
        gain_attend,
        gain_ffn,
        gain_post,
    ) = mats
    (
        inputs,
        segment,
        cosine,
        sine_part,
        normed,
        query_raw,
        key_raw,
        values,
        queries,
        keys_rot,
        kept_probs,
        attended,
        branch,
        middle,
        normed_two,
        gate_out,
        upward,
        hidden,
        branch_two,
    ) = kept
    grad_out = incoming.astype(jnp.float32)
    unused, pull_post = jax.vjp(norm_rows, branch_two, gain_post.astype(jnp.float32))
    d_branch_two, g_post = pull_post(grad_out)
    d_branch_two = d_branch_two.astype(jnp.bfloat16)
    gw_down = jnp.einsum("lf,ld->fd", hidden, d_branch_two, preferred_element_type=jnp.float32)
    d_hidden = jnp.einsum("ld,fd->lf", d_branch_two, w_down, preferred_element_type=jnp.float32)
    unused, pull_glu = jax.vjp(glu_part, gate_out, upward)
    d_gate, d_up = pull_glu(d_hidden)
    d_gate = d_gate.astype(jnp.bfloat16)
    d_up = d_up.astype(jnp.bfloat16)
    gw_gate = jnp.einsum("ld,lf->df", normed_two, d_gate, preferred_element_type=jnp.float32)
    gw_up = jnp.einsum("ld,lf->df", normed_two, d_up, preferred_element_type=jnp.float32)
    d_normed_two = jnp.einsum(
        "lf,df->ld", d_gate, w_gate, preferred_element_type=jnp.float32
    ) + jnp.einsum("lf,df->ld", d_up, w_up, preferred_element_type=jnp.float32)
    unused, pull_ffn = jax.vjp(norm_rows, middle, gain_ffn.astype(jnp.float32))
    d_mid_part, g_ffn = pull_ffn(d_normed_two)
    d_middle = grad_out + d_mid_part
    return (d_middle, (gw_gate, gw_up, gw_down, g_ffn, g_post))


def backward_attn(kept, d_middle, mats):
    (
        w_query,
        w_key,
        w_value,
        w_output,
        w_gate,
        w_up,
        w_down,
        gain_input,
        gain_query,
        gain_key,
        gain_attend,
        gain_ffn,
        gain_post,
    ) = mats
    (
        inputs,
        segment,
        cosine,
        sine_part,
        normed,
        query_raw,
        key_raw,
        values,
        queries,
        keys_rot,
        kept_probs,
        attended,
        branch,
        middle,
        normed_two,
        gate_out,
        upward,
        hidden,
        branch_two,
    ) = kept
    length = inputs.shape[0]
    width = w_key.shape[1]
    heads = w_query.shape[1] // width
    block = min(BLOCK, length)
    unused, pull_attend = jax.vjp(norm_rows, branch, gain_attend.astype(jnp.float32))
    d_branch, g_attend = pull_attend(d_middle)
    d_branch = d_branch.astype(jnp.bfloat16)
    gw_output = jnp.einsum("la,ld->ad", attended, d_branch, preferred_element_type=jnp.float32)
    d_attended = jnp.einsum("ld,ad->la", d_branch, w_output, preferred_element_type=jnp.float32)
    d_attended = d_attended.astype(jnp.bfloat16).reshape(length, heads, width)
    attended_heads = attended.reshape(length, heads, width)
    delta = jnp.sum(
        d_attended.astype(jnp.float32) * attended_heads.astype(jnp.float32), axis=-1
    ).T
    d_keys = [0.0] * (length // block)
    d_values = [0.0] * (length // block)
    d_query_parts = []
    for number, start in enumerate(range(0, length, block)):
        low = max(0, start - DOC_MOST)
        high = start + block
        rows_q = queries[start:high]
        rows_d = d_attended[start:high]
        probabilities = kept_probs[number]
        value_term = jnp.einsum(
            "hlm,lhd->md", probabilities, rows_d, preferred_element_type=jnp.float32
        )
        d_probs = jnp.einsum(
            "lhd,md->hlm", rows_d, values[low:high], preferred_element_type=jnp.float32
        )
        d_scores = probabilities.astype(jnp.float32) * (d_probs - delta[:, start:high, None])
        d_scores = d_scores.astype(jnp.bfloat16)
        d_query_parts.append(
            jnp.einsum(
                "hlm,md->lhd", d_scores, keys_rot[low:high], preferred_element_type=jnp.float32
            )
        )
        key_term = jnp.einsum("hlm,lhd->md", d_scores, rows_q, preferred_element_type=jnp.float32)
        for part in range(low // block, high // block):
            rows = slice(part * block - low, part * block - low + block)
            d_keys[part] = d_keys[part] + key_term[rows]
            d_values[part] = d_values[part] + value_term[rows]
    d_queries = jnp.concatenate(d_query_parts, axis=0)
    d_keys = jnp.concatenate(d_keys, axis=0)
    d_values = jnp.concatenate(d_values, axis=0)

    def query_map(raw_query, gain_value):
        return rotary(
            norm_rows(raw_query, gain_value), cosine[:, None, :], sine_part[:, None, :]
        ) * width ** (-0.5)

    def key_map(raw_key, gain_value):
        return rotary(norm_rows(raw_key, gain_value), cosine, sine_part)

    unused, pull_query = jax.vjp(query_map, query_raw, gain_query.astype(jnp.float32))
    d_query_raw, g_query = pull_query(d_queries)
    d_query_raw = d_query_raw.astype(jnp.bfloat16).reshape(length, heads * width)
    unused, pull_key = jax.vjp(key_map, key_raw, gain_key.astype(jnp.float32))
    d_key_raw, g_key = pull_key(d_keys)
    d_key_raw = d_key_raw.astype(jnp.bfloat16)
    d_values = d_values.astype(jnp.bfloat16)
    gw_query = jnp.einsum("ld,lq->dq", normed, d_query_raw, preferred_element_type=jnp.float32)
    gw_key = jnp.einsum("ld,lq->dq", normed, d_key_raw, preferred_element_type=jnp.float32)
    gw_value = jnp.einsum("ld,lq->dq", normed, d_values, preferred_element_type=jnp.float32)
    d_normed = (
        jnp.einsum("lq,dq->ld", d_query_raw, w_query, preferred_element_type=jnp.float32)
        + jnp.einsum("lq,dq->ld", d_key_raw, w_key, preferred_element_type=jnp.float32)
        + jnp.einsum("lq,dq->ld", d_values, w_value, preferred_element_type=jnp.float32)
    )
    unused, pull_input = jax.vjp(norm_rows, inputs, gain_input.astype(jnp.float32))
    d_in_part, g_input = pull_input(d_normed)
    grad_inputs = d_middle + d_in_part
    return (grad_inputs, (gw_query, gw_key, gw_value, gw_output, g_input, g_query, g_key, g_attend))


def flip_bit(size, bit):
    return [(i, i ^ (1 << bit)) for i in range(size)]


def half_axis(shape):
    if shape[1] % 256 == 0:
        return 1
    if shape[0] % 2 == 0:
        return 0
    return 1


def halves(x, axis):
    half = x.shape[axis] // 2
    return (
        lax.slice_in_dim(x, 0, half, axis=axis),
        lax.slice_in_dim(x, half, 2 * half, axis=axis),
    )


def exchange_sum(x, name, size, bit, axis):
    upper = ((lax.axis_index(name) >> bit) & 1) == 1
    low, high = halves(x, axis)
    away = lax.ppermute(jnp.where(upper, low, high), name, flip_bit(size, bit))
    kept = jnp.where(upper, high, low)
    return (kept.astype(jnp.float32) + away.astype(jnp.float32)).astype(x.dtype)


def exchange_join(x, name, size, bit, axis):
    upper = ((lax.axis_index(name) >> bit) & 1) == 1
    other = lax.ppermute(x, name, flip_bit(size, bit))
    return jnp.concatenate(
        [jnp.where(upper, other, x), jnp.where(upper, x, other)], axis=axis
    )


def bit_count(size):
    count = size.bit_length() - 1
    assert size == 1 << count
    return count


def gather_rows(x, size):
    for bit in range(bit_count(size)):
        x = exchange_join(x, "shard", size, bit, 0)
    return x


def sum_all(parts, shards, replicas):
    parts = list(parts)
    for bit in reversed(range(bit_count(shards))):
        parts = [exchange_sum(x, "shard", shards, bit, 0) for x in parts]
    count = bit_count(replicas)
    orders = []
    for number in range(len(parts)):
        base = list(range(count - 1))
        turn = number % max(len(base), 1)
        orders.append(base[turn:] + base[:turn] + [count - 1])
    done = [[] for _ in parts]
    for step in range(count):
        for number in range(len(parts)):
            axis = half_axis(parts[number].shape)
            done[number].append((orders[number][step], axis))
            parts[number] = exchange_sum(
                parts[number], "rep", replicas, orders[number][step], axis
            )
    for step in reversed(range(count)):
        for number in range(len(parts)):
            bit, axis = done[number][step]
            parts[number] = exchange_join(parts[number], "rep", replicas, bit, axis)
    return parts


def per_device(
    shards,
    replicas,
    tokens,
    segments,
    w_query,
    w_key,
    w_value,
    w_output,
    w_gate,
    w_up,
    w_down,
    gain_input,
    gain_query,
    gain_key,
    gain_attend,
    gain_ffn,
    gain_post,
    cotangent,
):
    queries_wide = w_query.shape[1]
    width = w_key.shape[1]
    w_all = gather_rows(jnp.concatenate([w_query, w_key, w_value], axis=1), shards)
    owned_gains = (gain_input, gain_attend, gain_ffn, gain_post, gain_query, gain_key)
    packed = gather_rows(jnp.concatenate(owned_gains)[None], shards)
    gains = []
    place = 0
    for gain in owned_gains:
        gains.append(packed[:, place : place + gain.shape[0]].reshape(-1))
        place += gain.shape[0]
    mats = (
        w_all[:, :queries_wide],
        w_all[:, queries_wide : queries_wide + width],
        w_all[:, queries_wide + width :],
        lax.all_gather(w_output, "shard", axis=0, tiled=True),
        lax.all_gather(w_gate, "shard", axis=0, tiled=True),
        lax.all_gather(w_up, "shard", axis=0, tiled=True),
        lax.all_gather(w_down, "shard", axis=0, tiled=True),
        gains[0],
        gains[4],
        gains[5],
        gains[1],
        gains[2],
        gains[3],
    )
    result, kept = forward(tokens[0].astype(jnp.float32), segments[0], mats)
    d_middle, ffn_terms = backward_ffn(kept, cotangent[0], mats)
    ffn_parts = [t.astype(jnp.bfloat16) for t in ffn_terms[:3]]
    d_middle, ffn_parts = lax.optimization_barrier((d_middle, ffn_parts))
    grad_gate, grad_up, grad_down = sum_all(ffn_parts, shards, replicas)
    grad_inputs, attn_terms = backward_attn(kept, d_middle, mats)
    g_query_w, g_key_w, g_value_w, g_output_w, g_input, g_query, g_key, g_attend = attn_terms
    g_ffn, g_post = ffn_terms[3:]

    gain_terms = (g_input, g_attend, g_ffn, g_post, g_query, g_key)
    small = jnp.concatenate([g.reshape(shards, -1) for g in gain_terms], axis=1)
    count = small.shape[1]
    rows = -(-count // (2 * width * 64)) * 64
    small = jnp.pad(small, ((0, 0), (0, rows * 2 * width - count)))
    small = small.reshape(shards, rows, 2 * width)
    key_value = jnp.concatenate([g_key_w, g_value_w], axis=1)
    own = key_value.shape[0] // shards
    key_value = jnp.concatenate([key_value.reshape(shards, own, 2 * width), small], axis=1)
    key_value = key_value.reshape(shards * (own + rows), 2 * width)
    attn_parts = [t.astype(jnp.bfloat16) for t in (g_query_w, g_output_w, key_value)]
    grad_query, grad_output, key_value = sum_all(attn_parts, shards, replicas)
    key_value = key_value.astype(jnp.float32)
    small = key_value[own:].reshape(-1)
    grad_gains = []
    place = 0
    for gain in owned_gains:
        grad_gains.append(small[place : place + gain.shape[0]])
        place += gain.shape[0]
    return (
        result.astype(jnp.bfloat16)[None],
        grad_inputs.astype(jnp.bfloat16)[None],
        grad_query.astype(jnp.float32),
        key_value[:own, :width],
        key_value[:own, width:],
        grad_output.astype(jnp.float32),
        grad_gate.astype(jnp.float32),
        grad_up.astype(jnp.float32),
        grad_down.astype(jnp.float32),
        grad_gains[0],
        grad_gains[4],
        grad_gains[5],
        grad_gains[1],
        grad_gains[2],
        grad_gains[3],
    )


def solution(mesh):
    in_specs = (
        P(("rep", "shard"), None, None),
        P(("rep", "shard"), None),
        P("shard", None),
        P("shard", None),
        P("shard", None),
        P("shard", None),
        P("shard", None),
        P("shard", None),
        P("shard", None),
        P("shard"),
        P("shard"),
        P("shard"),
        P("shard"),
        P("shard"),
        P("shard"),
        P(("rep", "shard"), None, None),
    )
    out_specs = (
        P(("rep", "shard"), None, None),
        P(("rep", "shard"), None, None),
        P("shard", None),
        P("shard", None),
        P("shard", None),
        P("shard", None),
        P("shard", None),
        P("shard", None),
        P("shard", None),
        P("shard"),
        P("shard"),
        P("shard"),
        P("shard"),
        P("shard"),
        P("shard"),
    )
    return jax.shard_map(
        functools.partial(per_device, mesh.shape["shard"], mesh.shape["rep"]),
        mesh=mesh, in_specs=in_specs, out_specs=out_specs, check_vma=False
    )
```

profile of v0, /device:TPU:0, one launch (start us, length us, event | category | flops | bytes accessed | tf_op | source)
XLA Modules:
  0.0 368.0 jit_solution(10880264214973401328)
XLA Ops:
  29.1 3.3 multiply_reduce_fusion.2
  46.7 3.4 fusion.172
  62.4 3.2 multiply_reduce_fusion.9
  68.5 8.9 %fusion.182 = f32[1024,2048]{1,0:T(8,128)} fusion(bf16[1024,640]{0,1:T(8,128)(2,1)} %multiply_convert_fusion.2, bf16[640,2048]{1,0:T(8,128)(2,1)} %all-gather.7.cloned.1.call-done), kind=kOutput, calls=%fused_computation.436 | convolution fusion | flops 2684354560 | bytes 12320768 | tf_op jit(solution)/shard_map/dot_general | solution.py:115
  77.4 11.3 %multiply_convert_fusion.1 = (bf16[1024,2048]{1,0:T(8,128)(2,1)}, f32[1024,2048]{1,0:T(8,128)}) fusion(f32[1024,2048]{1,0:T(8,128)} %fusion.182, bf16[1024,640]{0,1:T(8,128)(2,1)} %multiply_convert_fusion.2, bf16[640,2048]{1,0:T(8,128)(2,1)} %all-gather.9.cloned.1.call-done), kind=kOutput, calls=%fused_computation.14 | convolution fusion | flops 2705326080 | bytes 24903680 | tf_op jit(solution)/shard_map/dot_general | solution.py:116
  88.7 6.1 %multiply_reduce_fusion.7 = (f32[1024]{0:T(1024)S(1)}, f32[1024,640]{0,1:T(8,128)S(1)}) fusion(bf16[1024,2048]{1,0:T(8,128)(2,1)} %get-tuple-element.181, bf16[2048,640]{1,0:T(8,128)(2,1)} %all-gather.11.cloned.1.call-done), kind=kOutput, calls=%fused_computation.84 | convolution fusion | flops 2685664256 | bytes 9441280 | tf_op jit(solution)/shard_map/dot_general | solution.py:118
  99.0 4.9 %convolution_convert_fusion = bf16[2048,640]{1,0:T(8,128)(2,1)} fusion(bf16[1024,2048]{1,0:T(8,128)(2,1)S(1)} %copy-done.119, bf16[1024,640]{0,1:T(8,128)(2,1)S(1)} %get-tuple-element.75), kind=kOutput, calls=%fused_computation.42 | convolution fusion | flops 2685665280 | bytes 8126464 | tf_op jit(solution)/shard_map/lf,ld->fd/dot_general | solution.py:185
  104.0 12.6 %multiply_convert_fusion = (bf16[1024,2048]{1,0:T(8,128)(2,1)}, bf16[1024,2048]{1,0:T(8,128)(2,1)}) fusion(f32[1024,2048]{1,0:T(8,128)S(1)} %bitcast.373, f32[1024,2048]{1,0:T(8,128)} %get-tuple-element.182, bf16[1024,640]{0,1:T(8,128)(2,1)S(1)} %get-tuple-element.75, bf16[2048,640]{1,0:T(8,128)(2,1)S(1)} %copy-done.112), kind=kOutput, calls=%fused_computation.13 | convolution fusion | flops 2734686208 | bytes 29097984 | tf_op jit(solution)/shard_map/ld,fd->lf/dot_general | solution.py:186
  116.6 6.5 %convolution_convert_fusion.1 = bf16[640,2048]{1,0:T(8,128)(2,1)} fusion(bf16[1024,640]{0,1:T(8,128)(2,1)S(1)} %copy-done.51, bf16[1024,2048]{1,0:T(8,128)(2,1)} %get-tuple-element.69), kind=kOutput, calls=%fused_computation.43 | convolution fusion | flops 2685665280 | bytes 8126464 | tf_op jit(solution)/shard_map/ld,lf->df/dot_general | solution.py:192
  123.1 4.3 %convolution_convert_fusion.2 = bf16[640,2048]{1,0:T(8,128)(2,1)} fusion(bf16[1024,640]{0,1:T(8,128)(2,1)S(1)} %copy-done.51, bf16[1024,2048]{1,0:T(8,128)(2,1)S(1)} %copy-done.118), kind=kOutput, calls=%fused_computation.44 | convolution fusion | flops 2685665280 | bytes 8126464 | tf_op jit(solution)/shard_map/ld,lf->df/dot_general | solution.py:191
  127.5 3.0 fusion.183
  130.5 3.9 %multiply_reduce_fusion.3 = (bf16[640]{0:T(1024)(128)(2,1)}, f32[1024]{0:T(1024)S(1)}, f32[1024,640]{0,1:T(8,128)S(1)}) fusion(f32[1024,640]{0,1:T(8,128)S(1)} %get-tuple-element.68, f32[1024]{0:T(1024)S(1)} %fusion.127, f32[640]{0:T(1024)S(1)} %copy-done.78, f32[1024,640]{0,1:T(8,128)S(1)} %fusion.183, bf16[1024,2048]{1,0:T(8,128)(2,1)S(1)} %copy-done.117, ...), kind=kOutput, calls=%fused_computation.78 | convolution fusion | flops 2688940544 | bytes 14692096 | tf_op jit(solution)/shard_map/lf,df->ld/dot_general | solution.py:195
  194.3 3.8 %collective-permute-done.12 = bf16[384,256]{1,0:T(8,128)(2,1)S(1)} collective-permute-done((bf16[384,256]{1,0:T(8,128)(2,1)S(1)}, bf16[384,256]{1,0:T(8,128)(2,1)S(1)}, u32[]{:S(2)}, u32[]{:S(2)}) %collective-permute-start.12) | collective-permute-done | bytes 196640 | tf_op jit(solution)/shard_map/ppermute | solution.py:336
  222.3 6.2 %collective-permute-done.17 = bf16[192,128]{1,0:T(8,128)(2,1)S(1)} collective-permute-done((bf16[192,128]{1,0:T(8,128)(2,1)S(1)}, bf16[192,128]{1,0:T(8,128)(2,1)S(1)}, u32[]{:S(2)}, u32[]{:S(2)}) %collective-permute-start.17) | collective-permute-done | bytes 49184 | tf_op jit(solution)/shard_map/ppermute | solution.py:343
  230.1 4.1 %collective-permute-done.18 = bf16[384,128]{1,0:T(8,128)(2,1)S(1)} collective-permute-done((bf16[384,128]{1,0:T(8,128)(2,1)S(1)}, bf16[384,128]{1,0:T(8,128)(2,1)S(1)}, u32[]{:S(2)}, u32[]{:S(2)}) %collective-permute-start.18) | collective-permute-done | bytes 98336 | tf_op jit(solution)/shard_map/ppermute | solution.py:343
  237.8 3.4 collective-permute-done.3
  278.9 3.7 %collective-permute-done.27 = bf16[128,640]{1,0:T(8,128)(2,1)S(1)} collective-permute-done((bf16[128,640]{1,0:T(8,128)(2,1)S(1)}, bf16[128,640]{1,0:T(8,128)(2,1)S(1)}, u32[]{:S(2)}, u32[]{:S(2)}) %collective-permute-start.27) | collective-permute-done | bytes 163872 | tf_op jit(solution)/shard_map/ppermute | solution.py:343
  283.2 4.1 %collective-permute-done.9 = bf16[320,256]{1,0:T(8,128)(2,1)S(1)} collective-permute-done((bf16[320,256]{1,0:T(8,128)(2,1)S(1)}, bf16[320,256]{1,0:T(8,128)(2,1)S(1)}, u32[]{:S(2)}, u32[]{:S(2)}) %collective-permute-start.9) | collective-permute-done | bytes 163872 | tf_op jit(solution)/shard_map/ppermute | solution.py:343
  292.1 5.6 %collective-permute-done.10 = bf16[320,512]{1,0:T(8,128)(2,1)S(1)} collective-permute-done((bf16[320,512]{1,0:T(8,128)(2,1)S(1)}, bf16[320,512]{1,0:T(8,128)(2,1)S(1)}, u32[]{:S(2)}, u32[]{:S(2)}) %collective-permute-start.10) | collective-permute-done | bytes 327712 | tf_op jit(solution)/shard_map/ppermute | solution.py:343
  301.7 4.8 %collective-permute-done.49 = bf16[256,640]{1,0:T(8,128)(2,1)S(1)} collective-permute-done((bf16[256,640]{1,0:T(8,128)(2,1)S(1)}, bf16[256,640]{1,0:T(8,128)(2,1)S(1)}, u32[]{:S(2)}, u32[]{:S(2)}) %collective-permute-start.49) | collective-permute-done | bytes 327712 | tf_op jit(solution)/shard_map/ppermute | solution.py:336
  312.1 4.6 %collective-permute-start.51 = (bf16[64,640]{1,0:T(8,128)(2,1)S(1)}, bf16[64,640]{1,0:T(8,128)(2,1)S(1)}, u32[]{:S(2)}, u32[]{:S(2)}) collective-permute-start(bf16[64,640]{1,0:T(8,128)(2,1)S(1)} %broadcast_select_fusion.54), channel_id=1, source_target_pairs={{0,16},{2,18},{4,20},{6,22},{8,24},{10,26},{12,28},{14,30},{16,0},... | collective-permute-start | bytes 245768 | tf_op jit(solution)/shard_map/ppermute | solution.py:336
  335.7 3.3 collective-permute-start.45
  339.5 4.7 %collective-permute-done.54 = bf16[256,640]{1,0:T(8,128)(2,1)S(1)} collective-permute-done((bf16[256,640]{1,0:T(8,128)(2,1)S(1)}, bf16[256,640]{1,0:T(8,128)(2,1)S(1)}, u32[]{:S(2)}, u32[]{:S(2)}) %collective-permute-start.54) | collective-permute-done | bytes 327712 | tf_op jit(solution)/shard_map/ppermute | solution.py:343
  348.1 7.0 %collective-permute-done.55 = bf16[512,640]{1,0:T(8,128)(2,1)S(1)} collective-permute-done((bf16[512,640]{1,0:T(8,128)(2,1)S(1)}, bf16[512,640]{1,0:T(8,128)(2,1)S(1)}, u32[]{:S(2)}, u32[]{:S(2)}) %collective-permute-start.55) | collective-permute-done | bytes 655392 | tf_op jit(solution)/shard_map/ppermute | solution.py:343
  (597 shorter events, 224.9 us)
Async XLA Ops:
  7.3 55.1 %all-gather.5.cloned.1.call-start = ((), (), s32[]{:S(2)}) async-start(), calls=%async_computation | async-start | bytes 1966080 | tf_op jit(solution)/shard_map/all_gather | solution.py:420
  8.0 60.4 %all-gather.7.cloned.1.call-start = ((), (), s32[]{:S(2)}) async-start(), calls=%async_computation.1 | async-start | bytes 3932160 | tf_op jit(solution)/shard_map/all_gather | solution.py:421
  8.8 68.6 %all-gather.9.cloned.1.call-start = ((), (), s32[]{:S(2)}) async-start(), calls=%async_computation.2 | async-start | bytes 3932160 | tf_op jit(solution)/shard_map/all_gather | solution.py:422
  9.5 79.2 %all-gather.11.cloned.1.call-start = ((), (), s32[]{:S(2)}) async-start(), calls=%async_computation.3 | async-start | bytes 3932160 | tf_op jit(solution)/shard_map/all_gather | solution.py:423
  9.7 10.0 %collective-permute-start = (bf16[1,1536]{1,0:T(2,128)(2,1)S(1)}, bf16[1,1536]{1,0:T(2,128)(2,1)S(1)}, u32[]{:S(2)}, u32[]{:S(2)}) collective-permute-start(bf16[1,1536]{1,0:T(2,128)(2,1)S(1)} %broadcast_in_dim.64), channel_id=1, source_target_pairs={{0,1},{1,0},{2,3},{3,2},{4,5},{5,4},{6,7},{7,6},{8,9},{9,8},{10,11... | collective-permute-start | bytes 9224 | tf_op jit(solution)/shard_map/ppermute | solution.py:343
  10.3 12.2 %collective-permute-start.1 = (bf16[320,1536]{1,0:T(8,128)(2,1)S(1)}, bf16[320,1536]{1,0:T(8,128)(2,1)}, u32[]{:S(2)}, u32[]{:S(2)}) collective-permute-start(bf16[320,1536]{1,0:T(8,128)(2,1)S(1)} %constant_dynamic-update-slice_fusion), channel_id=1, source_target_pairs={{0,1},{1,0},{2,3},{3,2},{4,5},{5,4},{6,7},{7,6},{8,9},{9,8},{10,11... | collective-permute-start | bytes 2949128 | tf_op jit(solution)/shard_map/ppermute | solution.py:343
  185.4 81.6 %collective-permute-start.47 = (bf16[1024,640]{1,0:T(8,128)(2,1)}, bf16[1024,640]{1,0:T(8,128)(2,1)}, u32[]{:S(2)}, u32[]{:S(2)}) collective-permute-start(bf16[1024,640]{1,0:T(8,128)(2,1)} %broadcast_select_fusion), channel_id=1, source_target_pairs={{0,1},{1,0},{2,3},{3,2},{4,5},{5,4},{6,7},{7,6},{8,9},{9,8},{10,11... | collective-permute-start | bytes 3932168 | tf_op jit(solution)/shard_map/ppermute | solution.py:336
  186.8 82.3 %collective-permute-start.38 = (bf16[320,2048]{1,0:T(8,128)(2,1)}, bf16[320,2048]{1,0:T(8,128)(2,1)}, u32[]{:S(2)}, u32[]{:S(2)}) collective-permute-start(bf16[320,2048]{1,0:T(8,128)(2,1)} %broadcast_select_fusion.1), channel_id=1, source_target_pairs={{0,1},{1,0},{2,3},{3,2},{4,5},{5,4},{6,7},{7,6},{8,9},{9,8},{10,11... | collective-permute-start | bytes 3932168 | tf_op jit(solution)/shard_map/ppermute | solution.py:336
  188.9 83.2 %collective-permute-start.29 = (bf16[320,2048]{1,0:T(8,128)(2,1)}, bf16[320,2048]{1,0:T(8,128)(2,1)}, u32[]{:S(2)}, u32[]{:S(2)}) collective-permute-start(bf16[320,2048]{1,0:T(8,128)(2,1)} %broadcast_select_fusion.2), channel_id=1, source_target_pairs={{0,1},{1,0},{2,3},{3,2},{4,5},{5,4},{6,7},{7,6},{8,9},{9,8},{10,11... | collective-permute-start | bytes 3932168 | tf_op jit(solution)/shard_map/ppermute | solution.py:336
  189.1 20.8 %collective-permute-start.20 = (bf16[512,640]{1,0:T(8,128)(2,1)S(1)}, bf16[512,640]{1,0:T(8,128)(2,1)}, u32[]{:S(2)}, u32[]{:S(2)}) collective-permute-start(bf16[512,640]{1,0:T(8,128)(2,1)S(1)} %broadcast_select_fusion.14), channel_id=1, source_target_pairs={{0,1},{1,0},{2,3},{3,2},{4,5},{5,4},{6,7},{7,6},{8,9},{9,8},{10,11... | collective-permute-start | bytes 1966088 | tf_op jit(solution)/shard_map/ppermute | solution.py:336
  209.8 10.1 %collective-permute-start.2 = (bf16[320,1024]{1,0:T(8,128)(2,1)}, bf16[320,1024]{1,0:T(8,128)(2,1)S(1)}, u32[]{:S(2)}, u32[]{:S(2)}) collective-permute-start(bf16[320,1024]{1,0:T(8,128)(2,1)} %broadcast_select_fusion.15), channel_id=1, source_target_pairs={{0,1},{1,0},{2,3},{3,2},{4,5},{5,4},{6,7},{7,6},{8,9},{9,8},{10,11... | collective-permute-start | bytes 1966088 | tf_op jit(solution)/shard_map/ppermute | solution.py:336
  219.8 15.9 %collective-permute-start.21 = (bf16[256,640]{1,0:T(8,128)(2,1)S(1)}, bf16[256,640]{1,0:T(8,128)(2,1)S(1)}, u32[]{:S(2)}, u32[]{:S(2)}) collective-permute-start(bf16[256,640]{1,0:T(8,128)(2,1)S(1)} %broadcast_select_fusion.27), channel_id=1, source_target_pairs={{0,4},{2,6},{4,0},{6,2},{8,12},{10,14},{12,8},{14,10},{16,20},{18,... | collective-permute-start | bytes 983048 | tf_op jit(solution)/shard_map/ppermute | solution.py:336
  261.9 13.8 %collective-permute-start.26 = (bf16[64,640]{1,0:T(8,128)(2,1)S(1)}, bf16[64,640]{1,0:T(8,128)(2,1)S(1)}, u32[]{:S(2)}, u32[]{:S(2)}) collective-permute-start(bf16[64,640]{1,0:T(8,128)(2,1)S(1)} %pad_maximum_fusion.32), channel_id=1, source_target_pairs={{0,2},{2,0},{4,6},{6,4},{8,10},{10,8},{12,14},{14,12},{16,18},{18,... | collective-permute-start | bytes 245768 | tf_op jit(solution)/shard_map/ppermute | solution.py:343
  264.5 13.1 %collective-permute-start.8 = (bf16[320,128]{1,0:T(8,128)(2,1)S(1)}, bf16[320,128]{1,0:T(8,128)(2,1)S(1)}, u32[]{:S(2)}, u32[]{:S(2)}) collective-permute-start(bf16[320,128]{1,0:T(8,128)(2,1)S(1)} %pad_maximum_fusion.31), channel_id=1, source_target_pairs={{0,8},{2,10},{4,12},{6,14},{8,0},{10,2},{12,4},{14,6},{16,24},{18,... | collective-permute-start | bytes 245768 | tf_op jit(solution)/shard_map/ppermute | solution.py:343
  268.9 30.1 %collective-permute-start.48 = (bf16[512,640]{1,0:T(8,128)(2,1)S(1)}, bf16[512,640]{1,0:T(8,128)(2,1)S(1)}, u32[]{:S(2)}, u32[]{:S(2)}) collective-permute-start(bf16[512,640]{1,0:T(8,128)(2,1)S(1)} %broadcast_select_fusion.7), channel_id=1, source_target_pairs={{0,8},{2,10},{4,12},{6,14},{8,0},{10,2},{12,4},{14,6},{16,24},{18,... | collective-permute-start | bytes 1966088 | tf_op jit(solution)/shard_map/ppermute | solution.py:336
  271.4 28.5 %collective-permute-start.39 = (bf16[320,1024]{1,0:T(8,128)(2,1)S(1)}, bf16[320,1024]{1,0:T(8,128)(2,1)S(1)}, u32[]{:S(2)}, u32[]{:S(2)}) collective-permute-start(bf16[320,1024]{1,0:T(8,128)(2,1)S(1)} %broadcast_select_fusion.10), channel_id=1, source_target_pairs={{0,4},{2,6},{4,0},{6,2},{8,12},{10,14},{12,8},{14,10},{16,20},{18,... | collective-permute-start | bytes 1966088 | tf_op jit(solution)/shard_map/ppermute | solution.py:336
  274.2 26.8 %collective-permute-start.30 = (bf16[320,1024]{1,0:T(8,128)(2,1)S(1)}, bf16[320,1024]{1,0:T(8,128)(2,1)S(1)}, u32[]{:S(2)}, u32[]{:S(2)}) collective-permute-start(bf16[320,1024]{1,0:T(8,128)(2,1)S(1)} %broadcast_select_fusion.13), channel_id=1, source_target_pairs={{0,2},{2,0},{4,6},{6,4},{8,10},{10,8},{12,14},{14,12},{16,18},{18,... | collective-permute-start | bytes 1966088 | tf_op jit(solution)/shard_map/ppermute | solution.py:336
  277.6 9.7 %collective-permute-start.9 = (bf16[320,256]{1,0:T(8,128)(2,1)S(1)}, bf16[320,256]{1,0:T(8,128)(2,1)S(1)}, u32[]{:S(2)}, u32[]{:S(2)}) collective-permute-start(bf16[320,256]{1,0:T(8,128)(2,1)S(1)} %pad_maximum_fusion.21), channel_id=1, source_target_pairs={{0,4},{2,6},{4,0},{6,2},{8,12},{10,14},{12,8},{14,10},{16,20},{18,... | collective-permute-start | bytes 491528 | tf_op jit(solution)/shard_map/ppermute | solution.py:343
  287.4 10.3 %collective-permute-start.10 = (bf16[320,512]{1,0:T(8,128)(2,1)S(1)}, bf16[320,512]{1,0:T(8,128)(2,1)S(1)}, u32[]{:S(2)}, u32[]{:S(2)}) collective-permute-start(bf16[320,512]{1,0:T(8,128)(2,1)S(1)} %pad_maximum_fusion.15), channel_id=1, source_target_pairs={{0,2},{2,0},{4,6},{6,4},{8,10},{10,8},{12,14},{14,12},{16,18},{18,... | collective-permute-start | bytes 983048 | tf_op jit(solution)/shard_map/ppermute | solution.py:343
  333.5 10.7 %collective-permute-start.54 = (bf16[256,640]{1,0:T(8,128)(2,1)S(1)}, bf16[256,640]{1,0:T(8,128)(2,1)S(1)}, u32[]{:S(2)}, u32[]{:S(2)}) collective-permute-start(bf16[256,640]{1,0:T(8,128)(2,1)S(1)} %pad_maximum_fusion.19), channel_id=1, source_target_pairs={{0,2},{2,0},{4,6},{6,4},{8,10},{10,8},{12,14},{14,12},{16,18},{18,... | collective-permute-start | bytes 983048 | tf_op jit(solution)/shard_map/ppermute | solution.py:343
  335.7 10.2 %collective-permute-start.45 = (bf16[320,512]{1,0:T(8,128)(2,1)S(1)}, bf16[320,512]{1,0:T(8,128)(2,1)S(1)}, u32[]{:S(2)}, u32[]{:S(2)}) collective-permute-start(bf16[320,512]{1,0:T(8,128)(2,1)S(1)} %pad_maximum_fusion.18), channel_id=1, source_target_pairs={{0,8},{2,10},{4,12},{6,14},{8,0},{10,2},{12,4},{14,6},{16,24},{18,... | collective-permute-start | bytes 983048 | tf_op jit(solution)/shard_map/ppermute | solution.py:343
  344.4 10.7 %collective-permute-start.55 = (bf16[512,640]{1,0:T(8,128)(2,1)S(1)}, bf16[512,640]{1,0:T(8,128)(2,1)S(1)}, u32[]{:S(2)}, u32[]{:S(2)}) collective-permute-start(bf16[512,640]{1,0:T(8,128)(2,1)S(1)} %pad_maximum_fusion.6), channel_id=1, source_target_pairs={{0,8},{2,10},{4,12},{6,14},{8,0},{10,2},{12,4},{14,6},{16,24},{18,... | collective-permute-start | bytes 1966088 | tf_op jit(solution)/shard_map/ppermute | solution.py:343
  346.2 10.9 %collective-permute-start.46 = (bf16[320,1024]{1,0:T(8,128)(2,1)S(1)}, bf16[320,1024]{1,0:T(8,128)(2,1)S(1)}, u32[]{:S(2)}, u32[]{:S(2)}) collective-permute-start(bf16[320,1024]{1,0:T(8,128)(2,1)S(1)} %pad_maximum_fusion.5), channel_id=1, source_target_pairs={{0,4},{2,6},{4,0},{6,2},{8,12},{10,14},{12,8},{14,10},{16,20},{18,... | collective-permute-start | bytes 1966088 | tf_op jit(solution)/shard_map/ppermute | solution.py:343
  347.3 11.9 %collective-permute-start.37 = (bf16[320,1024]{1,0:T(8,128)(2,1)S(1)}, bf16[320,1024]{1,0:T(8,128)(2,1)S(1)}, u32[]{:S(2)}, u32[]{:S(2)}) collective-permute-start(bf16[320,1024]{1,0:T(8,128)(2,1)S(1)} %pad_maximum_fusion.4), channel_id=1, source_target_pairs={{0,2},{2,0},{4,6},{6,4},{8,10},{10,8},{12,14},{14,12},{16,18},{18,... | collective-permute-start | bytes 1966088 | tf_op jit(solution)/shard_map/ppermute | solution.py:343
  (159 other events, 794.2 us)
Sparse Core Ops, SparseCore 0:
  9.6 12.1 all-gather.4
  23.4 12.4 all-gather.6
  37.4 12.5 all-gather.8
  51.4 12.5 all-gather.10
where the time goes:
time: 374 us; the launch traced here: 368 us
  matrix products  108 us (29%)
  starting transfers between devices  77.1 us (21%)
  waiting for transfers between devices  67.1 us (18%)
  other arithmetic  66.4 us (18%)
  local copies, waits for them, and re-layouts  33.4 us (9%)
  between operations  16.3 us (4%)
    ppermute x26, waiting for transfers between devices, exchange_join(): other = lax.ppermute(x, name, flip_bit(size, bit))  45.8 us
    ppermute x30, starting transfers between devices, exchange_sum(): away = lax.ppermute(jnp.where(upper, low, high), name, flip_bit(size, bit))  38.5 us
    ppermute x26, starting transfers between devices, exchange_join(): other = lax.ppermute(x, name, flip_bit(size, bit))  38.5 us
    unnamed x252, local copies, waits for them, and re-layouts  24.2 us
    ppermute x30, waiting for transfers between devices, exchange_sum(): away = lax.ppermute(jnp.where(upper, low, high), name, flip_bit(size, bit))  19.2 us
    dot_general x1, matrix products, backward_ffn(): jnp.einsum('ld,fd->lf', d_branch_two, w_down, preferred_element_type=jnp....  12.6 us
    dot_general x1, matrix products, forward(): upward = jnp.dot(normed_two, w_up, preferred_element_type=jnp.float32)  11.3 us
    convert_element_type x30, other arithmetic, exchange_sum(): return (kept.astype(jnp.float32) + away.astype(jnp.float32)).astype(x.dtype)  10 us
  transfers between devices with their start and end apart: 60, of which 26 were waited for; matrix products, arithmetic and copies ran while one was open for 29% of the time, Pallas kernels for 0%

commit v1 on v0

--- a/solution.py
+++ b/solution.py
@@ -9,6 +9,7 @@
 THETA = 1000000.0
 BLOCK = 256
 DOC_MOST = 512
+TIED = (2,)
 
 
 def norm_rows(values, gain):
@@ -199,7 +200,7 @@
     return (d_middle, (gw_gate, gw_up, gw_down, g_ffn, g_post))
 
 
-def backward_attn(kept, d_middle, mats):
+def backward_attn(kept, d_middle, mats, begin):
     (
         w_query,
         w_key,
@@ -246,6 +247,10 @@
     gw_output = jnp.einsum("la,ld->ad", attended, d_branch, preferred_element_type=jnp.float32)
     d_attended = jnp.einsum("ld,ad->la", d_branch, w_output, preferred_element_type=jnp.float32)
     d_attended = d_attended.astype(jnp.bfloat16).reshape(length, heads, width)
+    d_attended, gw_output = lax.optimization_barrier(
+        (d_attended, gw_output.astype(jnp.bfloat16))
+    )
+    summing = begin(gw_output)
     attended_heads = attended.reshape(length, heads, width)
     delta = jnp.sum(
         d_attended.astype(jnp.float32) * attended_heads.astype(jnp.float32), axis=-1
@@ -257,6 +262,10 @@
         low = max(0, start - DOC_MOST)
         high = start + block
         rows_q = queries[start:high]
+        if number in TIED:
+            d_attended, d_query_parts, d_keys, d_values = summing.tie(
+                (d_attended, d_query_parts, d_keys, d_values)
+            )
         rows_d = d_attended[start:high]
         probabilities = kept_probs[number]
         value_term = jnp.einsum(
@@ -277,6 +286,7 @@
             rows = slice(part * block - low, part * block - low + block)
             d_keys[part] = d_keys[part] + key_term[rows]
             d_values[part] = d_values[part] + value_term[rows]
+    d_query_parts, d_keys, d_values = summing.tie((d_query_parts, d_keys, d_values))
     d_queries = jnp.concatenate(d_query_parts, axis=0)
     d_keys = jnp.concatenate(d_keys, axis=0)
     d_values = jnp.concatenate(d_values, axis=0)
@@ -296,6 +306,7 @@
     d_key_raw, g_key = pull_key(d_keys)
     d_key_raw = d_key_raw.astype(jnp.bfloat16)
     d_values = d_values.astype(jnp.bfloat16)
+    d_query_raw, d_key_raw, d_values = summing.tie((d_query_raw, d_key_raw, d_values))
     gw_query = jnp.einsum("ld,lq->dq", normed, d_query_raw, preferred_element_type=jnp.float32)
     gw_key = jnp.einsum("ld,lq->dq", normed, d_key_raw, preferred_element_type=jnp.float32)
     gw_value = jnp.einsum("ld,lq->dq", normed, d_values, preferred_element_type=jnp.float32)
@@ -307,7 +318,7 @@
     unused, pull_input = jax.vjp(norm_rows, inputs, gain_input.astype(jnp.float32))
     d_in_part, g_input = pull_input(d_normed)
     grad_inputs = d_middle + d_in_part
-    return (grad_inputs, (gw_query, gw_key, gw_value, gw_output, g_input, g_query, g_key, g_attend))
+    return (grad_inputs, summing, (gw_query, gw_key, gw_value, g_input, g_query, g_key, g_attend))
 
 
 def flip_bit(size, bit):
@@ -358,10 +369,11 @@
     return x
 
 
-def sum_all(parts, shards, replicas):
+def sum_stages(parts, shards, replicas):
     parts = list(parts)
     for bit in reversed(range(bit_count(shards))):
         parts = [exchange_sum(x, "shard", shards, bit, 0) for x in parts]
+    parts = yield parts
     count = bit_count(replicas)
     orders = []
     for number in range(len(parts)):
@@ -376,11 +388,31 @@
             parts[number] = exchange_sum(
                 parts[number], "rep", replicas, orders[number][step], axis
             )
+        parts = yield parts
     for step in reversed(range(count)):
         for number in range(len(parts)):
             bit, axis = done[number][step]
             parts[number] = exchange_join(parts[number], "rep", replicas, bit, axis)
-    return parts
+        parts = yield parts
+
+
+class Summing:
+    def __init__(self, parts, shards, replicas):
+        self.stages = sum_stages(parts, shards, replicas)
+        self.left = 1 + 2 * bit_count(replicas)
+        self.parts = next(self.stages)
+        self.left -= 1
+
+    def advance(self):
+        if self.left:
+            self.parts = list(self.stages.send(self.parts))
+            self.left -= 1
+
+    def tie(self, value):
+        value, self.parts = lax.optimization_barrier((value, self.parts))
+        self.parts = list(self.parts)
+        self.advance()
+        return value
 
 
 def per_device(
@@ -432,23 +464,46 @@
     d_middle, ffn_terms = backward_ffn(kept, cotangent[0], mats)
     ffn_parts = [t.astype(jnp.bfloat16) for t in ffn_terms[:3]]
     d_middle, ffn_parts = lax.optimization_barrier((d_middle, ffn_parts))
-    grad_gate, grad_up, grad_down = sum_all(ffn_parts, shards, replicas)
-    grad_inputs, attn_terms = backward_attn(kept, d_middle, mats)
-    g_query_w, g_key_w, g_value_w, g_output_w, g_input, g_query, g_key, g_attend = attn_terms
+
+    def begin(grad_output):
+        rows_all = jnp.concatenate(
+            [x.reshape(shards, -1, x.shape[1]) for x in (ffn_parts[2], grad_output)], axis=1
+        ).reshape(-1, grad_output.shape[1])
+        return Summing(ffn_parts[:2] + [rows_all], shards, replicas)
+
+    ffn_parts = list(ffn_parts)
+    grad_inputs, early, attn_terms = backward_attn(kept, d_middle, mats, begin)
+    g_query_w, g_key_w, g_value_w, g_input, g_query, g_key, g_attend = attn_terms
     g_ffn, g_post = ffn_terms[3:]
 
     gain_terms = (g_input, g_attend, g_ffn, g_post, g_query, g_key)
     small = jnp.concatenate([g.reshape(shards, -1) for g in gain_terms], axis=1)
     count = small.shape[1]
-    rows = -(-count // (2 * width * 64)) * 64
+    rows = -(-count // (2 * width * 16)) * 16
     small = jnp.pad(small, ((0, 0), (0, rows * 2 * width - count)))
     small = small.reshape(shards, rows, 2 * width)
     key_value = jnp.concatenate([g_key_w, g_value_w], axis=1)
     own = key_value.shape[0] // shards
     key_value = jnp.concatenate([key_value.reshape(shards, own, 2 * width), small], axis=1)
     key_value = key_value.reshape(shards * (own + rows), 2 * width)
-    attn_parts = [t.astype(jnp.bfloat16) for t in (g_query_w, g_output_w, key_value)]
-    grad_query, grad_output, key_value = sum_all(attn_parts, shards, replicas)
+    wide = g_query_w.reshape(shards, own, queries_wide)
+    wide = jnp.pad(wide, ((0, 0), (0, rows), (0, 0)))
+    wide = wide.reshape(shards * (own + rows), queries_wide)
+    attn_parts = [jnp.concatenate([wide, key_value], axis=1).astype(jnp.bfloat16)]
+    attn_parts = early.tie(attn_parts)
+    late = Summing(attn_parts, shards, replicas)
+    while late.left:
+        if early.left:
+            late.parts = list(early.tie(late.parts))
+        late.advance()
+    while early.left:
+        early.advance()
+    grad_gate, grad_up, rows_all = early.parts
+    down_rows = ffn_parts[2].shape[0] // shards
+    grad_down, grad_output = rows_all[:down_rows], rows_all[down_rows:]
+    late_sum = late.parts[0]
+    grad_query = late_sum[:own, :queries_wide]
+    key_value = late_sum[:, queries_wide:]
     key_value = key_value.astype(jnp.float32)
     small = key_value[own:].reshape(-1)
     grad_gains = []

time: 374 us -> 367 us (0.981)
  starting transfers between devices: 77.1 us -> 43.9 us
  other arithmetic: 66.4 us -> 75.8 us
  matrix products: 108 us -> 114 us
  waiting for transfers between devices: 67.1 us -> 71.8 us
  local copies, waits for them, and re-layouts: 33.4 us -> 37.9 us
    ppermute x26 -> x18, starting transfers between devices: 38.5 us -> 19.5 us  [exchange_join(): other = lax.ppermute(x, name, flip_bit(size, bit))]
    ppermute x30 -> x20, waiting for transfers between devices: 19.2 us -> 34.5 us  [exchange_sum(): away = lax.ppermute(jnp.where(upper, low, high), name, flip_bit(size, bit))]
    ppermute x30 -> x20, starting transfers between devices: 38.5 us -> 24.2 us  [exchange_sum(): away = lax.ppermute(jnp.where(upper, low, high), name, flip_bit(size, bit))]
    ppermute x26 -> x18, waiting for transfers between devices: 45.8 us -> 35.2 us  [exchange_join(): other = lax.ppermute(x, name, flip_bit(size, bit))]
    convert_element_type x30 -> x20, other arithmetic: 10 us -> 13.5 us  [exchange_sum(): return (kept.astype(jnp.float32) + away.astype(jnp.float32)).astype(x.dtype)]
  transfers between devices with their start and end apart: 60 -> 42, of which waited for: 26 -> 20; matrix products, arithmetic and copies ran while one was open for 29% -> 40% of each run, Pallas kernels for 0% -> 0%
where the time goes in v1:
time: 367 us; the launch traced here: 360 us
  matrix products  114 us (31%)
  other arithmetic  75.8 us (21%)
  waiting for transfers between devices  71.8 us (20%)
  starting transfers between devices  43.9 us (12%)
  local copies, waits for them, and re-layouts  37.9 us (10%)
  between operations  16.3 us (4%)
    ppermute x18, waiting for transfers between devices, exchange_join(): other = lax.ppermute(x, name, flip_bit(size, bit))  35.2 us
    ppermute x20, waiting for transfers between devices, exchange_sum(): away = lax.ppermute(jnp.where(upper, low, high), name, flip_bit(size, bit))  34.5 us
    unnamed x252, local copies, waits for them, and re-layouts  25.7 us
    ppermute x20, starting transfers between devices, exchange_sum(): away = lax.ppermute(jnp.where(upper, low, high), name, flip_bit(size, bit))  24.2 us
    ppermute x18, starting transfers between devices, exchange_join(): other = lax.ppermute(x, name, flip_bit(size, bit))  19.5 us
    dot_general x1, matrix products, backward_ffn(): jnp.einsum('ld,fd->lf', d_branch_two, w_down, preferred_element_type=jnp....  15.1 us
    convert_element_type x20, other arithmetic, exchange_sum(): return (kept.astype(jnp.float32) + away.astype(jnp.float32)).astype(x.dtype)  13.5 us
    dot_general x1, matrix products, forward(): upward = jnp.dot(normed_two, w_up, preferred_element_type=jnp.float32)  11.2 us
  transfers between devices with their start and end apart: 42, of which 20 were waited for; matrix products, arithmetic and copies ran while one was open for 40% of the time, Pallas kernels for 0%

profile of v1, /device:TPU:0, one launch (start us, length us, event | category | flops | bytes accessed | tf_op | source)
XLA Modules:
  0.0 360.1 jit_solution(16376532741587049990)
XLA Ops:
  29.5 3.4 multiply_reduce_fusion.3
  68.2 3.5 multiply_reduce_fusion.10
  76.1 9.0 %fusion.182 = f32[1024,2048]{1,0:T(8,128)} fusion(bf16[1024,640]{0,1:T(8,128)(2,1)} %multiply_convert_fusion.2, bf16[640,2048]{1,0:T(8,128)(2,1)} %all-gather.7.cloned.1.call-done), kind=kOutput, calls=%fused_computation.406 | convolution fusion | flops 2684354560 | bytes 12320768 | tf_op jit(solution)/shard_map/dot_general | solution.py:116
  85.1 11.2 %multiply_convert_fusion.1 = (bf16[1024,2048]{1,0:T(8,128)(2,1)}, f32[1024,2048]{1,0:T(8,128)}) fusion(f32[1024,2048]{1,0:T(8,128)} %fusion.182, bf16[1024,640]{0,1:T(8,128)(2,1)} %multiply_convert_fusion.2, bf16[640,2048]{1,0:T(8,128)(2,1)} %all-gather.9.cloned.1.call-done), kind=kOutput, calls=%fused_computation.14 | convolution fusion | flops 2705326080 | bytes 24903680 | tf_op jit(solution)/shard_map/dot_general | solution.py:117
  96.3 5.7 %multiply_reduce_fusion.8 = (f32[1024]{0:T(1024)S(1)}, f32[1024,640]{0,1:T(8,128)S(1)}) fusion(bf16[1024,2048]{1,0:T(8,128)(2,1)} %get-tuple-element.279, bf16[2048,640]{1,0:T(8,128)(2,1)} %all-gather.11.cloned.1.call-done), kind=kOutput, calls=%fused_computation.86 | convolution fusion | flops 2685664256 | bytes 9441280 | tf_op jit(solution)/shard_map/dot_general | solution.py:119
  106.5 3.7 %convolution_convert_fusion = bf16[2048,640]{1,0:T(8,128)(2,1)S(1)} fusion(bf16[1024,2048]{1,0:T(8,128)(2,1)S(1)} %copy-done.119, bf16[1024,640]{0,1:T(8,128)(2,1)S(1)} %get-tuple-element.190), kind=kOutput, calls=%fused_computation.45 | convolution fusion | flops 2685665280 | bytes 8126464 | tf_op jit(solution)/shard_map/lf,ld->fd/dot_general | solution.py:186
  110.3 15.1 %multiply_convert_fusion = (bf16[1024,2048]{1,0:T(8,128)(2,1)S(1)}, bf16[1024,2048]{1,0:T(8,128)(2,1)}) fusion(f32[1024,2048]{1,0:T(8,128)} %fusion.182, f32[1024,2048]{1,0:T(8,128)} %get-tuple-element.280, bf16[1024,640]{0,1:T(8,128)(2,1)S(1)} %get-tuple-element.190, bf16[2048,640]{1,0:T(8,128)(2,1)S(1)} %copy-done.116), kind=kOutput, calls=%fused_computation.13 | convolution fusion | flops 2734686208 | bytes 29097984 | tf_op jit(solution)/shard_map/ld,fd->lf/dot_general | solution.py:187
  128.5 3.3 convolution_convert_fusion.2
  134.8 3.4 multiply_reduce_fusion.4
  168.1 4.6 %fusion.13 = bf16[1536,640]{1,0:T(8,128)(2,1)S(1)} fusion(bf16[1536,640]{1,0:T(8,128)(2,1)} %collective-permute-done.4, pred[]{:T(512)S(6)} %eq.58, bf16[2,512,640]{2,1,0:T(8,128)(2,1)S(1)} %bitcast.329, bf16[2,1024,640]{2,1,0:T(8,128)(2,1)S(1)} %bitcast.325), kind=kLoop, calls=%fused_computation.30 | loop fusion | flops 12779520 | bytes 7864321 | tf_op jit(solution)/shard_map/convert_element_type | solution.py:349
  176.4 3.2 collective-permute-start.7
  186.4 9.9 %collective-permute-done.6 = bf16[320,1024]{1,0:T(8,128)(2,1)S(1)} collective-permute-done((bf16[320,1024]{1,0:T(8,128)(2,1)S(1)}, bf16[320,1024]{1,0:T(8,128)(2,1)S(1)}, u32[]{:S(2)}, u32[]{:S(2)}) %collective-permute-start.6) | collective-permute-done | bytes 655392 | tf_op jit(solution)/shard_map/ppermute | solution.py:347
  198.0 3.7 %collective-permute-done.7 = bf16[768,640]{1,0:T(8,128)(2,1)S(1)} collective-permute-done((bf16[768,640]{1,0:T(8,128)(2,1)S(1)}, bf16[768,640]{1,0:T(8,128)(2,1)S(1)}, u32[]{:S(2)}, u32[]{:S(2)}) %collective-permute-start.7) | collective-permute-done | bytes 983072 | tf_op jit(solution)/shard_map/ppermute | solution.py:347
  231.1 3.3 fusion.91
  250.8 6.7 %collective-permute-done.16 = bf16[320,128]{1,0:T(8,128)(2,1)S(1)} collective-permute-done((bf16[320,128]{1,0:T(8,128)(2,1)S(1)}, bf16[320,128]{1,0:T(8,128)(2,1)S(1)}, u32[]{:S(2)}, u32[]{:S(2)}) %collective-permute-start.16) | collective-permute-done | bytes 81952 | tf_op jit(solution)/shard_map/ppermute | solution.py:347
  264.5 9.0 %collective-permute-done.20 = bf16[320,128]{1,0:T(8,128)(2,1)S(1)} collective-permute-done((bf16[320,128]{1,0:T(8,128)(2,1)S(1)}, bf16[320,128]{1,0:T(8,128)(2,1)S(1)}, u32[]{:S(2)}, u32[]{:S(2)}) %collective-permute-start.20) | collective-permute-done | bytes 81952 | tf_op jit(solution)/shard_map/ppermute | solution.py:354
  285.2 3.8 %collective-permute-done.22 = bf16[336,384]{1,0:T(8,128)(2,1)S(1)} collective-permute-done((bf16[336,384]{1,0:T(8,128)(2,1)S(1)}, bf16[336,384]{1,0:T(8,128)(2,1)S(1)}, u32[]{:S(2)}, u32[]{:S(2)}) %collective-permute-start.22) | collective-permute-done | bytes 258080 | tf_op jit(solution)/shard_map/ppermute | solution.py:347
  295.7 4.1 %collective-permute-done.28 = bf16[320,512]{1,0:T(8,128)(2,1)S(1)} collective-permute-done((bf16[320,512]{1,0:T(8,128)(2,1)S(1)}, bf16[320,512]{1,0:T(8,128)(2,1)S(1)}, u32[]{:S(2)}, u32[]{:S(2)}) %collective-permute-start.28) | collective-permute-done | bytes 327712 | tf_op jit(solution)/shard_map/ppermute | solution.py:354
  304.2 6.0 %collective-permute-done.30 = bf16[84,384]{1,0:T(8,128)(2,1)S(1)} collective-permute-done((bf16[84,384]{1,0:T(8,128)(2,1)S(1)}, bf16[84,384]{1,0:T(8,128)(2,1)S(1)}, u32[]{:S(2)}, u32[]{:S(2)}) %collective-permute-start.30) | collective-permute-done | bytes 64544 | tf_op jit(solution)/shard_map/ppermute | solution.py:347
  311.8 3.7 %collective-permute-done.31 = bf16[84,384]{1,0:T(8,128)(2,1)S(1)} collective-permute-done((bf16[84,384]{1,0:T(8,128)(2,1)S(1)}, bf16[84,384]{1,0:T(8,128)(2,1)S(1)}, u32[]{:S(2)}, u32[]{:S(2)}) %collective-permute-start.31) | collective-permute-done | bytes 64544 | tf_op jit(solution)/shard_map/ppermute | solution.py:354
  317.2 3.4 collective-permute-done.32
  322.8 3.2 fusion.60
  329.3 3.5 collective-permute-done.33
  338.7 5.6 %collective-permute-done.36 = bf16[320,1024]{1,0:T(8,128)(2,1)S(1)} collective-permute-done((bf16[320,1024]{1,0:T(8,128)(2,1)}, bf16[320,1024]{1,0:T(8,128)(2,1)S(1)}, u32[]{:S(2)}, u32[]{:S(2)}) %collective-permute-start.36) | collective-permute-done | bytes 655392 | tf_op jit(solution)/shard_map/ppermute | solution.py:354
  (533 shorter events, 211.5 us)
Async XLA Ops:
  7.3 61.0 %all-gather.5.cloned.1.call-start = ((), (), s32[]{:S(2)}) async-start(), calls=%async_computation | async-start | bytes 1966080 | tf_op jit(solution)/shard_map/all_gather | solution.py:452
  8.0 68.1 %all-gather.7.cloned.1.call-start = ((), (), s32[]{:S(2)}) async-start(), calls=%async_computation.1 | async-start | bytes 3932160 | tf_op jit(solution)/shard_map/all_gather | solution.py:453
  8.8 76.3 %all-gather.9.cloned.1.call-start = ((), (), s32[]{:S(2)}) async-start(), calls=%async_computation.2 | async-start | bytes 3932160 | tf_op jit(solution)/shard_map/all_gather | solution.py:454
  9.5 86.8 %all-gather.11.cloned.1.call-start = ((), (), s32[]{:S(2)}) async-start(), calls=%async_computation.3 | async-start | bytes 3932160 | tf_op jit(solution)/shard_map/all_gather | solution.py:455
  149.4 18.7 %collective-permute-start.4 = (bf16[1536,640]{1,0:T(8,128)(2,1)}, bf16[1536,640]{1,0:T(8,128)(2,1)}, u32[]{:S(2)}, u32[]{:S(2)}) collective-permute-start(bf16[1536,640]{1,0:T(8,128)(2,1)} %select_bitcast_fusion), channel_id=1, source_target_pairs={{0,1},{1,0},{2,3},{3,2},{4,5},{5,4},{6,7},{7,6},{8,9},{9,8},{10,11... | collective-permute-start | bytes 5898248 | tf_op jit(solution)/shard_map/ppermute | solution.py:347
  151.1 12.7 %collective-permute-start.3 = (bf16[320,2048]{1,0:T(8,128)(2,1)}, bf16[320,2048]{1,0:T(8,128)(2,1)}, u32[]{:S(2)}, u32[]{:S(2)}) collective-permute-start(bf16[320,2048]{1,0:T(8,128)(2,1)} %broadcast_select_fusion), channel_id=1, source_target_pairs={{0,1},{1,0},{2,3},{3,2},{4,5},{5,4},{6,7},{7,6},{8,9},{9,8},{10,11... | collective-permute-start | bytes 3932168 | tf_op jit(solution)/shard_map/ppermute | solution.py:347
  176.4 25.3 %collective-permute-start.7 = (bf16[768,640]{1,0:T(8,128)(2,1)S(1)}, bf16[768,640]{1,0:T(8,128)(2,1)S(1)}, u32[]{:S(2)}, u32[]{:S(2)}) collective-permute-start(bf16[768,640]{1,0:T(8,128)(2,1)S(1)} %broadcast_select_fusion.5), channel_id=1, source_target_pairs={{0,8},{2,10},{4,12},{6,14},{8,0},{10,2},{12,4},{14,6},{16,24},{18,... | collective-permute-start | bytes 2949128 | tf_op jit(solution)/shard_map/ppermute | solution.py:347
  179.7 16.6 %collective-permute-start.6 = (bf16[320,1024]{1,0:T(8,128)(2,1)S(1)}, bf16[320,1024]{1,0:T(8,128)(2,1)S(1)}, u32[]{:S(2)}, u32[]{:S(2)}) collective-permute-start(bf16[320,1024]{1,0:T(8,128)(2,1)S(1)} %broadcast_select_fusion.10), channel_id=1, source_target_pairs={{0,4},{2,6},{4,0},{6,2},{8,12},{10,14},{12,8},{14,10},{16,20},{18,... | collective-permute-start | bytes 1966088 | tf_op jit(solution)/shard_map/ppermute | solution.py:347
  181.3 16.3 %collective-permute-start.5 = (bf16[320,1024]{1,0:T(8,128)(2,1)S(1)}, bf16[320,1024]{1,0:T(8,128)(2,1)S(1)}, u32[]{:S(2)}, u32[]{:S(2)}) collective-permute-start(bf16[320,1024]{1,0:T(8,128)(2,1)S(1)} %broadcast_select_fusion.13), channel_id=1, source_target_pairs={{0,2},{2,0},{4,6},{6,4},{8,10},{10,8},{12,14},{14,12},{16,18},{18,... | collective-permute-start | bytes 1966088 | tf_op jit(solution)/shard_map/ppermute | solution.py:347
  202.2 17.5 %collective-permute-start.10 = (bf16[384,640]{1,0:T(8,128)(2,1)S(1)}, bf16[384,640]{1,0:T(8,128)(2,1)S(1)}, u32[]{:S(2)}, u32[]{:S(2)}) collective-permute-start(bf16[384,640]{1,0:T(8,128)(2,1)S(1)} %broadcast_select_fusion.19), channel_id=1, source_target_pairs={{0,2},{2,0},{4,6},{6,4},{8,10},{10,8},{12,14},{14,12},{16,18},{18,... | collective-permute-start | bytes 1474568 | tf_op jit(solution)/shard_map/ppermute | solution.py:347
  204.0 15.3 %collective-permute-start.9 = (bf16[320,512]{1,0:T(8,128)(2,1)S(1)}, bf16[320,512]{1,0:T(8,128)(2,1)S(1)}, u32[]{:S(2)}, u32[]{:S(2)}) collective-permute-start(bf16[320,512]{1,0:T(8,128)(2,1)S(1)} %broadcast_select_fusion.22), channel_id=1, source_target_pairs={{0,8},{2,10},{4,12},{6,14},{8,0},{10,2},{12,4},{14,6},{16,24},{18,... | collective-permute-start | bytes 983048 | tf_op jit(solution)/shard_map/ppermute | solution.py:347
  205.7 13.9 %collective-permute-start.8 = (bf16[320,512]{1,0:T(8,128)(2,1)S(1)}, bf16[320,512]{1,0:T(8,128)(2,1)S(1)}, u32[]{:S(2)}, u32[]{:S(2)}) collective-permute-start(bf16[320,512]{1,0:T(8,128)(2,1)S(1)} %broadcast_select_fusion.25), channel_id=1, source_target_pairs={{0,4},{2,6},{4,0},{6,2},{8,12},{10,14},{12,8},{14,10},{16,20},{18,... | collective-permute-start | bytes 983048 | tf_op jit(solution)/shard_map/ppermute | solution.py:347
  224.6 20.0 %collective-permute-start.13 = (bf16[192,640]{1,0:T(8,128)(2,1)}, bf16[192,640]{1,0:T(8,128)(2,1)S(1)}, u32[]{:S(2)}, u32[]{:S(2)}) collective-permute-start(bf16[192,640]{1,0:T(8,128)(2,1)} %broadcast_select_fusion.31), channel_id=1, source_target_pairs={{0,4},{2,6},{4,0},{6,2},{8,12},{10,14},{12,8},{14,10},{16,20},{18,... | collective-permute-start | bytes 737288 | tf_op jit(solution)/shard_map/ppermute | solution.py:347
  225.8 16.0 %collective-permute-start.12 = (bf16[320,256]{1,0:T(8,128)(2,1)}, bf16[320,256]{1,0:T(8,128)(2,1)}, u32[]{:S(2)}, u32[]{:S(2)}) collective-permute-start(bf16[320,256]{1,0:T(8,128)(2,1)} %broadcast_select_fusion.34), channel_id=1, source_target_pairs={{0,2},{2,0},{4,6},{6,4},{8,10},{10,8},{12,14},{14,12},{16,18},{18,... | collective-permute-start | bytes 491528 | tf_op jit(solution)/shard_map/ppermute | solution.py:347
  227.1 16.5 %collective-permute-start.11 = (bf16[320,256]{1,0:T(8,128)(2,1)}, bf16[320,256]{1,0:T(8,128)(2,1)}, u32[]{:S(2)}, u32[]{:S(2)}) collective-permute-start(bf16[320,256]{1,0:T(8,128)(2,1)} %broadcast_select_fusion.37), channel_id=1, source_target_pairs={{0,8},{2,10},{4,12},{6,14},{8,0},{10,2},{12,4},{14,6},{16,24},{18,... | collective-permute-start | bytes 491528 | tf_op jit(solution)/shard_map/ppermute | solution.py:347
  244.8 14.2 %collective-permute-start.17 = (bf16[96,640]{1,0:T(8,128)(2,1)S(1)}, bf16[96,640]{1,0:T(8,128)(2,1)S(1)}, u32[]{:S(2)}, u32[]{:S(2)}) collective-permute-start(bf16[96,640]{1,0:T(8,128)(2,1)S(1)} %broadcast_select_fusion.43), channel_id=1, source_target_pairs={{0,16},{2,18},{4,20},{6,22},{8,24},{10,26},{12,28},{14,30},{16,0},... | collective-permute-start | bytes 368648 | tf_op jit(solution)/shard_map/ppermute | solution.py:347
  259.7 15.7 %collective-permute-start.21 = (bf16[96,640]{1,0:T(8,128)(2,1)S(1)}, bf16[96,640]{1,0:T(8,128)(2,1)S(1)}, u32[]{:S(2)}, u32[]{:S(2)}) collective-permute-start(bf16[96,640]{1,0:T(8,128)(2,1)S(1)} %add_convert_fusion.16), channel_id=1, source_target_pairs={{0,16},{2,18},{4,20},{6,22},{8,24},{10,26},{12,28},{14,30},{16,0},... | collective-permute-start | bytes 368648 | tf_op jit(solution)/shard_map/ppermute | solution.py:354
  259.7 13.8 %collective-permute-start.20 = (bf16[320,128]{1,0:T(8,128)(2,1)S(1)}, bf16[320,128]{1,0:T(8,128)(2,1)S(1)}, u32[]{:S(2)}, u32[]{:S(2)}) collective-permute-start(bf16[320,128]{1,0:T(8,128)(2,1)S(1)} %add_convert_fusion.17), channel_id=1, source_target_pairs={{0,16},{2,18},{4,20},{6,22},{8,24},{10,26},{12,28},{14,30},{16,0},... | collective-permute-start | bytes 245768 | tf_op jit(solution)/shard_map/ppermute | solution.py:354
  262.7 12.6 %collective-permute-start.19 = (bf16[320,128]{1,0:T(8,128)(2,1)S(1)}, bf16[320,128]{1,0:T(8,128)(2,1)S(1)}, u32[]{:S(2)}, u32[]{:S(2)}) collective-permute-start(bf16[320,128]{1,0:T(8,128)(2,1)S(1)} %add_convert_fusion.18), channel_id=1, source_target_pairs={{0,16},{2,18},{4,20},{6,22},{8,24},{10,26},{12,28},{14,30},{16,0},... | collective-permute-start | bytes 245768 | tf_op jit(solution)/shard_map/ppermute | solution.py:354
  262.8 13.0 %collective-permute-start.18 = (bf16[336,768]{1,0:T(8,128)(2,1)S(1)}, bf16[336,768]{1,0:T(8,128)(2,1)S(1)}, u32[]{:S(2)}, u32[]{:S(2)}) collective-permute-start(bf16[336,768]{1,0:T(8,128)(2,1)S(1)} %broadcast_select_fusion.16), channel_id=1, source_target_pairs={{0,2},{2,0},{4,6},{6,4},{8,10},{10,8},{12,14},{14,12},{16,18},{18,... | collective-permute-start | bytes 1548296 | tf_op jit(solution)/shard_map/ppermute | solution.py:347
  315.7 20.0 %collective-permute-start.37 = (bf16[320,1024]{1,0:T(8,128)(2,1)S(1)}, bf16[320,1024]{1,0:T(8,128)(2,1)}, u32[]{:S(2)}, u32[]{:S(2)}) collective-permute-start(bf16[320,1024]{1,0:T(8,128)(2,1)S(1)} %pad_maximum_fusion.10), channel_id=1, source_target_pairs={{0,4},{2,6},{4,0},{6,2},{8,12},{10,14},{12,8},{14,10},{16,20},{18,... | collective-permute-start | bytes 1966088 | tf_op jit(solution)/shard_map/ppermute | solution.py:354
  327.5 18.7 %collective-permute-start.35 = (bf16[768,640]{1,0:T(8,128)(2,1)}, bf16[768,640]{1,0:T(8,128)(2,1)S(1)}, u32[]{:S(2)}, u32[]{:S(2)}) collective-permute-start(bf16[768,640]{1,0:T(8,128)(2,1)} %pad_maximum_fusion.5), channel_id=1, source_target_pairs={{0,8},{2,10},{4,12},{6,14},{8,0},{10,2},{12,4},{14,6},{16,24},{18,... | collective-permute-start | bytes 2949128 | tf_op jit(solution)/shard_map/ppermute | solution.py:354
  327.5 16.7 %collective-permute-start.36 = (bf16[320,1024]{1,0:T(8,128)(2,1)}, bf16[320,1024]{1,0:T(8,128)(2,1)S(1)}, u32[]{:S(2)}, u32[]{:S(2)}) collective-permute-start(bf16[320,1024]{1,0:T(8,128)(2,1)} %pad_maximum_fusion.9), channel_id=1, source_target_pairs={{0,2},{2,0},{4,6},{6,4},{8,10},{10,8},{12,14},{14,12},{16,18},{18,... | collective-permute-start | bytes 1966088 | tf_op jit(solution)/shard_map/ppermute | solution.py:354
  333.9 15.9 %collective-permute-start.34 = (bf16[336,768]{1,0:T(8,128)(2,1)S(1)}, bf16[336,768]{1,0:T(8,128)(2,1)S(1)}, u32[]{:S(2)}, u32[]{:S(2)}) collective-permute-start(bf16[336,768]{1,0:T(8,128)(2,1)S(1)} %pad_maximum_fusion.13), channel_id=1, source_target_pairs={{0,2},{2,0},{4,6},{6,4},{8,10},{10,8},{12,14},{14,12},{16,18},{18,... | collective-permute-start | bytes 1548296 | tf_op jit(solution)/shard_map/ppermute | solution.py:354
  (141 other events, 708.2 us)
Sparse Core Ops, SparseCore 0:
  9.6 12.1 all-gather.4
  23.3 12.5 all-gather.6
  37.4 12.5 all-gather.8
  51.4 12.5 all-gather.10
